TPU v7x, 128 devices: a whole 4x4x4 slice. The times are simulated.
128 devices in a mesh: dp: 64 (over y, z_hi, x, core), tower: 2 (over z_lo).
Axes of the slice: x: 4, y: 4, z: 4 (z_hi: 2, z_lo: 2; z = z_hi * 2 + z_lo), core: 2. Of those that a mesh axis runs over, the one named last changes fastest.
Arguments:
- image: bfloat16 [65536, 1152], P('dp', 'tower'), may hold values from -0.19921875 to 0.19921875
- text: bfloat16 [65536, 1152], P('dp', 'tower'), may hold values from -0.19921875 to 0.19921875
- scale: float32 [], replicated, may hold values from 3 to 8
- bias: float32 [], replicated, may hold values from -3 to -1
- table: int32 [3, 64], replicated, may hold values from 0 to 63, as said below
- labels: int32 [64, 1024], P('dp'), may hold values from 0 to 1023, each once within a row
Outputs:
- image_grad: float32 [65536, 1152], P('dp', 'tower')
- text_grad: float32 [65536, 1152], P('dp', 'tower')
Inputs may be any that keep to these rules, and one draw needn't show every extreme that they name: For every round k there is a bit number b_k with table[k, d] = d xor 2^b_k for every d; the b_k of the 3 rounds are distinct. Each block's row of labels holds every number of 0 to 1023 once.
All inputs are finite; a program needn't handle non-finite values.
Results may differ from a plain program's by a relative error of at most 0.0043.
Values may be sent and summed in bfloat16 or wider, within the bound.
A program may use at most 192 MiB of HBM per device.

v0:
```python
from functools import partial

import jax
import jax.numpy as jnp
from jax import lax
from jax.sharding import PartitionSpec as P


def as_sent(array):
    return jax.tree.map(lambda a: a.astype(jnp.bfloat16) if a.dtype == jnp.float32 else a, array)


def from_partner_2(array, axis, distance):
    return lax.ppermute(array, axis, [(i, i ^ 1 << distance) for i in range(lax.axis_size(axis))])


def to_partner(rows, bit_number):
    return jax.tree.map(
        lambda part, own: part.astype(own.dtype),
        from_partner_2(as_sent(rows), "dp", bit_number),
        rows,
    )


def from_partner(rows, bit_number):
    return from_partner_2(rows, "dp", bit_number)


def summed_tile(tile):
    return lax.psum(tile, "tower")


def per_device(image, text, scale, bias, table, labels):
    wide_image = image.astype(jnp.float32)
    wide_text = text.astype(jnp.float32)
    image_sq, text_sq = lax.psum(
        (jnp.sum(wide_image * wide_image, axis=1), jnp.sum(wide_text * wide_text, axis=1)), "tower"
    )
    inverse_image = lax.rsqrt(image_sq + 1e-06)[:, None]
    inverse_text = lax.rsqrt(text_sq + 1e-06)[:, None]
    unit_image = wide_image * inverse_image
    unit_text = wide_text * inverse_text
    normed_image = unit_image.astype(jnp.bfloat16)
    normed_text = unit_text.astype(jnp.bfloat16)
    row_count = image.shape[0]
    columns = jnp.arange(row_count, dtype=jnp.int32)
    positive = (columns[None, :] == labels[0][:, None]).astype(jnp.float32)

    def similarity(text_half):
        return summed_tile(jnp.dot(normed_image, text_half.T, preferred_element_type=jnp.float32))

    own_weight = (jax.nn.sigmoid(scale * similarity(normed_text) + bias) - positive).astype(
        jnp.bfloat16
    )
    grad_image = jnp.dot(own_weight, normed_text, preferred_element_type=jnp.float32)
    grad_text = jnp.dot(own_weight.T, normed_image, preferred_element_type=jnp.float32)
    bit_count = lax.axis_size("dp").bit_length() - 1
    for round_index in range(table.shape[0]):
        mask = table[round_index, 0]
        which_bit = sum(
            (jnp.where(mask == 1 << position, position, 0) for position in range(bit_count))
        ).astype(jnp.int32)
        senders = [partial(to_partner, bit_number=position) for position in range(bit_count)]
        returners = [partial(from_partner, bit_number=position) for position in range(bit_count)]
        partner_text = lax.switch(which_bit, senders, normed_text)
        weight = jax.nn.sigmoid(scale * similarity(partner_text) + bias).astype(jnp.bfloat16)
        grad_image = grad_image + jnp.dot(weight, partner_text, preferred_element_type=jnp.float32)
        partner_term = jnp.dot(weight.T, normed_image, preferred_element_type=jnp.float32)
        grad_text = grad_text + lax.switch(which_bit, returners, partner_term)
    grad_image = scale * grad_image
    grad_text = scale * grad_text
    image_along, text_along = lax.psum(
        (jnp.sum(unit_image * grad_image, axis=1), jnp.sum(unit_text * grad_text, axis=1)), "tower"
    )
    image_grad = inverse_image * (grad_image - unit_image * image_along[:, None])
    text_grad = inverse_text * (grad_text - unit_text * text_along[:, None])
    return (image_grad, text_grad)


def solution(mesh):
    return jax.shard_map(
        per_device,
        mesh=mesh,
        in_specs=(P("dp", "tower"), P("dp", "tower"), P(), P(), P(), P("dp", None)),
        out_specs=(P("dp", "tower"), P("dp", "tower")),
        check_vma=False,
    )
```

profile of v0, /device:TPU:1, one launch (start us, length us, event | category | flops | bytes accessed | tf_op | source)
XLA Modules:
  0.0 660.4 jit_solution(17693434879169851085)
XLA Ops:
  7.2 0.0 copy-start
  7.2 0.0 all-reduce.5.cloned.1.call-start
  7.2 1.4 fusion.29
  18.2 0.0 copy-start.1
  18.2 1.6 fusion.13
  19.8 1.5 fusion.9
  21.4 4.8 all-reduce.1
  26.3 0.3 fusion.2
  26.6 4.3 conditional.7
  26.6 1.7 collective-permute-start.6
  28.2 2.6 collective-permute-done.6
  30.8 3.8 fusion.27
  34.6 5.1 fusion.23
  39.7 29.8 %conditional.6 = (bf16[1024,576]{0,1:T(8,128)(2,1)}) conditional(s32[]{:T(128)} %bitcast.1, bf16[1024,576]{0,1:T(8,128)(2,1)S(1)} %fusion.2, bf16[1024,576]{0,1:T(8,128)(2,1)S(1)} %fusion.2, bf16[1024,576]{0,1:T(8,128)(2,1)S(1)} %fusion.2, bf16[1024,576]{0,1:T(8,128)(2,1)S(1)} %fusion.2, ...), branch_computations={%region_5.6_spmd, %region_6.7_spmd, %region_7.8_spmd, %region_8.9_... | conditional | bytes 4718640 | solution.py:65
  39.7 3.7 collective-permute-start.3
  43.4 26.1 %collective-permute-done.3 = bf16[1024,576]{0,1:T(8,128)(2,1)} collective-permute-done((bf16[1024,576]{0,1:T(8,128)(2,1)S(1)}, bf16[1024,576]{0,1:T(8,128)(2,1)}, u32[]{:S(2)}, u32[]{:S(2)}) %collective-permute-start.3) | collective-permute-done | bytes 1179680 | tf_op jit(solution)/shard_map/cond/branch_3_fun/ppermute | solution.py:14
  69.6 5.1 fusion.25
  74.6 26.7 %conditional.8 = (bf16[1024,576]{0,1:T(8,128)(2,1)}) conditional(s32[]{:T(128)} %bitcast.3, bf16[1024,576]{0,1:T(8,128)(2,1)S(1)} %fusion.2, bf16[1024,576]{0,1:T(8,128)(2,1)S(1)} %fusion.2, bf16[1024,576]{0,1:T(8,128)(2,1)S(1)} %fusion.2, bf16[1024,576]{0,1:T(8,128)(2,1)S(1)} %fusion.2, ...), branch_computations={%region_19.20_spmd, %region_20.21_spmd, %region_21.22_spmd, %regio... | conditional | bytes 4718640 | solution.py:65
  74.6 1.2 collective-permute-start.13
  75.9 25.5 %collective-permute-done.13 = bf16[1024,576]{0,1:T(8,128)(2,1)} collective-permute-done((bf16[1024,576]{0,1:T(8,128)(2,1)S(1)}, bf16[1024,576]{0,1:T(8,128)(2,1)}, u32[]{:S(2)}, u32[]{:S(2)}) %collective-permute-start.13) | collective-permute-done | bytes 1179680 | tf_op jit(solution)/shard_map/cond/branch_1_fun/ppermute | solution.py:14
  101.4 5.1 fusion.21
  106.4 0.0 all-reduce.5.cloned.1.call-update
  107.8 388.8 %all-reduce.5.cloned.1.call-done = (f32[1024,1024]{1,0:T(8,128)}, f32[1024,1024]{1,0:T(8,128)}, f32[1024,1024]{1,0:T(8,128)}, f32[1024,1024]{1,0:T(8,128)}) async-done(((f32[1024,1024]{1,0:T(8,128)}, f32[1024,1024]{1,0:T(8,128)}, f32[1024,1024]{1,0:T(8,128)}, f32[1024,1024]{1,0:T(8,128)}), (f32[1024,1024]{1,0:T(8,128)}, f32[1024,1024]{1,0:T(8,128)}, f32[1024,1024]{1,0:T(8,128)}, ...) | async-done | bytes 16777232 | tf_op jit(solution)/shard_map/psum | solution.py:30
  496.5 3.3 divide_convert_fusion.2
  499.8 2.9 fusion.15
  502.7 4.3 fusion.31
  506.9 1.1 divide_convert_fusion.1
  508.1 1.4 fusion.17
  509.5 4.1 fusion.32
  513.6 5.0 conditional.10
  513.6 0.7 collective-permute-start.24
  514.2 4.3 collective-permute-done.24
  518.5 54.3 %conditional.9 = (f32[1024,576]{0,1:T(8,128)}) conditional(s32[]{:T(128)} %bitcast.1, f32[1024,576]{0,1:T(8,128)} %fusion.15, f32[1024,576]{0,1:T(8,128)} %fusion.15, f32[1024,576]{0,1:T(8,128)} %fusion.15, f32[1024,576]{0,1:T(8,128)} %fusion.15, f32[1024,576]{0,1:T(8,128)} %fusion.15, f32[1024,576]{0,1:T(8,128)} %fusion.15), branch_computations={%region_28.29_spmd, %region_29.30_spmd, %region_30.31_spmd, %regio... | conditional | bytes 9437232 | solution.py:69
  518.5 2.6 collective-permute-start.21
  521.1 51.7 %collective-permute-done.21 = f32[1024,576]{0,1:T(8,128)} collective-permute-done((f32[1024,576]{0,1:T(8,128)}, f32[1024,576]{0,1:T(8,128)}, u32[]{:S(2)}, u32[]{:S(2)}) %collective-permute-start.21) | collective-permute-done | bytes 2359328 | tf_op jit(solution)/shard_map/cond/branch_3_fun/ppermute | solution.py:14
  572.8 3.7 fusion.19
  576.5 51.7 %conditional.11 = (f32[1024,576]{0,1:T(8,128)}) conditional(s32[]{:T(128)} %bitcast.3, f32[1024,576]{0,1:T(8,128)S(1)} %fusion.19, f32[1024,576]{0,1:T(8,128)S(1)} %fusion.19, f32[1024,576]{0,1:T(8,128)S(1)} %fusion.19, f32[1024,576]{0,1:T(8,128)S(1)} %fusion.19, f32[1024,576]{0,1:T(8,128)S(1)} %fusion.19, ...), branch_computations={%region_40.41_spmd, %region_41.42_spmd, %region_42.43_spmd, %regio... | conditional | bytes 9437232 | solution.py:69
  576.6 1.3 collective-permute-start.31
  577.8 50.4 %collective-permute-done.31 = f32[1024,576]{0,1:T(8,128)} collective-permute-done((f32[1024,576]{0,1:T(8,128)S(1)}, f32[1024,576]{0,1:T(8,128)}, u32[]{:S(2)}, u32[]{:S(2)}) %collective-permute-start.31) | collective-permute-done | bytes 2359328 | tf_op jit(solution)/shard_map/cond/branch_1_fun/ppermute | solution.py:14
  628.3 3.2 subtract_convert_fusion
  631.5 1.4 fusion.30
  632.9 0.0 copy-start.6
  633.0 0.0 copy-start.7
  633.0 6.4 fusion.10
  639.4 4.7 fusion.6
  644.1 3.8 all-reduce
  647.9 3.8 fusion.12
  651.7 1.8 fusion.8
  (13 shorter events, 0.0 us)
Async XLA Ops:
  7.2 19.1 %copy-start = (bf16[1024,576]{0,1:T(8,128)(2,1)S(1)}, bf16[1024,576]{0,1:T(8,128)(2,1)}, u32[]{:S(2)}) copy-start(bf16[1024,576]{0,1:T(8,128)(2,1)} %param.43) | copy-start | bytes 3538948
  7.2 489.4 %all-reduce.5.cloned.1.call-start = ((), (), s32[]{:S(2)}) async-start(), calls=%async_computation | async-start | bytes 33554432 | tf_op jit(solution)/shard_map/psum | solution.py:30
  18.2 12.6 %copy-start.1 = (bf16[1024,576]{0,1:T(8,128)(2,1)S(1)}, bf16[1024,576]{0,1:T(8,128)(2,1)}, u32[]{:S(2)}) copy-start(bf16[1024,576]{0,1:T(8,128)(2,1)} %param.42) | copy-start | bytes 3538948
  26.6 4.3 collective-permute-start.6
  39.7 29.8 %collective-permute-start.3 = (bf16[1024,576]{0,1:T(8,128)(2,1)S(1)}, bf16[1024,576]{0,1:T(8,128)(2,1)}, u32[]{:S(2)}, u32[]{:S(2)}) collective-permute-start(bf16[1024,576]{0,1:T(8,128)(2,1)S(1)} %param.3), channel_id=1, source_target_pairs={{0,16},{2,18},{4,20},{6,22},{8,24},{10,26},{12,28},{14,30},{16,0},... | collective-permute-start | bytes 3538952 | tf_op jit(solution)/shard_map/cond/branch_3_fun/ppermute | solution.py:14
  74.6 26.7 %collective-permute-start.13 = (bf16[1024,576]{0,1:T(8,128)(2,1)S(1)}, bf16[1024,576]{0,1:T(8,128)(2,1)}, u32[]{:S(2)}, u32[]{:S(2)}) collective-permute-start(bf16[1024,576]{0,1:T(8,128)(2,1)S(1)} %param.13), channel_id=1, source_target_pairs={{0,4},{2,6},{4,0},{6,2},{8,12},{10,14},{12,8},{14,10},{16,20},{18,... | collective-permute-start | bytes 3538952 | tf_op jit(solution)/shard_map/cond/branch_1_fun/ppermute | solution.py:14
  502.7 4.3 copy-start.2
  513.6 5.0 collective-permute-start.24
  518.5 54.3 %collective-permute-start.21 = (f32[1024,576]{0,1:T(8,128)}, f32[1024,576]{0,1:T(8,128)}, u32[]{:S(2)}, u32[]{:S(2)}) collective-permute-start(f32[1024,576]{0,1:T(8,128)} %param.21), channel_id=1, source_target_pairs={{0,16},{2,18},{4,20},{6,22},{8,24},{10,26},{12,28},{14,30},{16,0},... | collective-permute-start | bytes 7077896 | tf_op jit(solution)/shard_map/cond/branch_3_fun/ppermute | solution.py:14
  572.8 55.5 %copy-start.4 = (s32[1,1024]{1,0:T(1,128)S(1)}, s32[1,1024]{1,0:T(1,128)}, u32[]{:S(2)}) copy-start(s32[1,1024]{1,0:T(1,128)} %param.47) | copy-start | bytes 12292
  576.6 51.7 %collective-permute-start.31 = (f32[1024,576]{0,1:T(8,128)S(1)}, f32[1024,576]{0,1:T(8,128)}, u32[]{:S(2)}, u32[]{:S(2)}) collective-permute-start(f32[1024,576]{0,1:T(8,128)S(1)} %param.31), channel_id=1, source_target_pairs={{0,4},{2,6},{4,0},{6,2},{8,12},{10,14},{12,8},{14,10},{16,20},{18,... | collective-permute-start | bytes 7077896 | tf_op jit(solution)/shard_map/cond/branch_1_fun/ppermute | solution.py:14
  632.9 6.4 copy-start.5
  632.9 6.4 copy-start.6
  633.0 6.4 copy-start.7
  647.9 3.8 copy-start.3
Sparse Core Ops, SparseCore 0:
  106.6 389.9 all-reduce.4
where the time goes:
time: 663 us; the launch traced here: 660 us
  waiting for transfers between devices  549 us (83%)
  matrix products  47.9 us (7%)
  between operations  25 us (4%)
  other arithmetic  16.7 us (3%)
  starting transfers between devices  11.1 us (2%)
  blocking collectives  8.66 us (1%)
    psum x1, waiting for transfers between devices, summed_tile(): return lax.psum(tile, 'tower')  389 us
    ppermute x6, waiting for transfers between devices, from_partner_2(): lax.ppermute(array, axis, [(i, i ^ 1 << distance) for i in range(lax.axis...  161 us
    dot_general x4, matrix products, similarity(): jnp.dot(normed_image, text_half.T, preferred_element_type=jnp.float32)  19.1 us
  transfers between devices with their start and end apart: 7, of which 7 were waited for; matrix products, arithmetic and copies ran while one was open for 0% of the time, Pallas kernels for 0%

commit v1 on v0

v1 whole, which is shorter than its diff:
```python
from functools import partial

import jax
import jax.numpy as jnp
from jax import lax
from jax.experimental import pallas as pl
from jax.experimental.pallas import tpu as pltpu
from jax.sharding import PartitionSpec as P

MESH = pl.DeviceIdType.MESH
BF = jnp.bfloat16
F32 = jnp.float32
NT = (((1,), (1,)), ((), ()))
WIDTH, DEPTH, ROWS = 1152, 576, 1024
CHUNK, TILE = 256, 512
SLOT_OF_BIT = (5, 1, 2, 6, 3, 4)
NEAR = (1, 3, 5)


def flip(index, bit):
    return index + (1 - 2 * ((index // (1 << bit)) % 2)) * (1 << bit)


def columns_of(half):
    return pl.ds(pl.multiple_of(DEPTH * half, DEPTH), DEPTH)


def rows_of(chunk):
    return pl.ds(CHUNK * chunk, CHUNK)


def kernel(
    table, scale_in, bias_in, labels_in, text_in, image_in, text_out, image_out,
    text_a, text_b, image_a, image_b, mine, q, kn, acc, gradient_out, labels, label_column,
    swap_s, swap_r, link_s, link_r, core_s, core_r, relay_s, last_s, last_r, label_s, label_r,
):
    me, a = lax.axis_index("dp"), lax.axis_index("tower")
    c = me % 2
    other = (c - a) * (c - a)
    sibling = (me + 1 - 2 * c, a)
    across = (me, 1 - a)
    diagonal = (me + 1 - 2 * c, 1 - a)
    home = (me - c + a, 1 - a)
    near = {1: (flip(me, 1), a), 3: (flip(me, 4), a), 5: across}
    beyond = {1: (flip(flip(me, 1), 2), a), 3: (flip(flip(me, 4), 5), a), 5: (flip(me, 3), 1 - a)}
    inputs, outputs = (text_in, image_in), (image_out, text_out)
    buffers = ((text_a, text_b), (image_a, image_b))

    barrier = pltpu.get_barrier_semaphore()
    peers = [sibling, across, diagonal, near[1], near[3], *beyond.values()]
    for peer in peers:
        pl.semaphore_signal(barrier, inc=1, device_id=peer, device_id_type=MESH)

    def remote(src, dst, send, recv, device):
        return pltpu.make_async_remote_copy(
            src_ref=src, dst_ref=dst, send_sem=send, recv_sem=recv, device_id=device, device_id_type=MESH
        )

    def place(slot, array, half, chunk):
        return buffers[array][chunk // 2].at[slot, columns_of(half), rows_of(chunk % 2)]

    def swap_copy(array, chunk):
        return remote(
            inputs[array].at[:, rows_of(chunk)], place(0, array, a, chunk),
            swap_s.at[array, chunk], swap_r.at[array, chunk], (me - c + a, c),
        )

    def swap_wait(array, chunk):
        remote(
            inputs[array].at[:, rows_of(chunk)], place(0, array, c, chunk),
            swap_s.at[array, chunk], swap_r.at[array, chunk], (me - c + a, c),
        ).wait_recv()

    def own_copy(array, chunk):
        return pltpu.make_async_copy(
            inputs[array].at[:, rows_of(chunk)], place(0, array, a, chunk), swap_r.at[array, chunk]
        )

    def beside_copy(array, chunk):
        return remote(
            inputs[array].at[:, rows_of(chunk)], place(5, array, a, chunk),
            link_s.at[2, array, chunk], link_r.at[4, array, chunk], sibling,
        )

    def link_copy(s, array, chunk):
        return remote(
            place(0, array, c, chunk), place(s, array, c, chunk),
            link_s.at[s // 2, array, chunk], link_r.at[s - 1, array, chunk], near[s],
        )

    def relay_copy(s, array, chunk):
        return remote(
            place(s, array, c, chunk), place(s + 1, array, c, chunk),
            relay_s.at[s // 2, array, chunk], link_r.at[s, array, chunk], beyond[s],
        )

    def core_copy(s, array, chunk, half):
        return remote(
            place(s, array, half, chunk), place(s, array, half, chunk),
            core_s.at[s, array, chunk], core_r.at[s, array, chunk], sibling,
        )

    def last_copy(array, half, device):
        return remote(
            gradient_out.at[array, columns_of(half), :],
            outputs[array].at[:, pl.ds(pl.multiple_of(TILE * c, TILE), TILE)],
            last_s.at[array, half], last_r.at[array, c], device,
        )

    def home_copy(array):
        return pltpu.make_async_copy(
            gradient_out.at[array, columns_of(a), :],
            outputs[array].at[:, pl.ds(pl.multiple_of(TILE * c, TILE), TILE)],
            last_r.at[array, c],
        )

    def pass_on(s, array, chunk):
        remote(
            place(0, array, c, chunk), place(s, array, c, chunk),
            link_s.at[0, array, chunk], link_r.at[s - 1, array, chunk], across,
        ).wait_recv()
        if s in NEAR:
            relay_copy(s, array, chunk).start()
        core_copy(s, array, chunk, c).start()

    def fan_out(array, chunk):
        link_copy(1, array, chunk).start()
        link_copy(3, array, chunk).start()
        core_copy(0, array, chunk, c).start()

    def pass_text(chunk):
        for s in (1, 3):
            pass_on(s, 0, chunk)
        if chunk > 0:
            for s in (2, 4):
                pass_on(s, 0, chunk - 1)

    chunks = [(array, chunk) for array in range(2) for chunk in range(4)]
    label_copy = remote(labels_in, labels, label_s, label_r, sibling)

    @pl.when(other == 0)
    def _():
        for which in chunks:
            own_copy(*which).start()

    pl.semaphore_wait(barrier, len(peers))

    @pl.when(other == 0)
    def _():
        for which in chunks:
            own_copy(*which).wait()
            fan_out(*which)
        label_copy.start()
        labels[...] = labels_in[...]
        for which in chunks:
            pass_on(5, *which)
        for chunk in range(4):
            pass_text(chunk)
        label_copy.wait_send()

    @pl.when(other == 1)
    def _():
        for which in chunks:
            swap_copy(*which).start()
        for which in chunks:
            beside_copy(*which).start()
        for n, which in enumerate(chunks):
            swap_wait(*which)
            fan_out(*which)
            if n > 0:
                pass_on(6, *chunks[n - 1])
            if n % 2 == 1:
                pass_text(n // 2)
        pass_on(6, *chunks[7])
        label_copy.wait_recv()

    for b in range(4):
        row = labels[0:1, pl.ds(pl.multiple_of(512 * c + 128 * b, 128), 128)].astype(F32)
        label_column[0, 128 * b : 128 * b + 128, :] = jnp.broadcast_to(row, (128, 128)).T
    row = labels[0:1, :].astype(F32)
    position = lax.broadcasted_iota(jnp.int32, (8, 1024), 1).astype(F32)

    def invert(n, carry):
        base = (512 * c + 8 * n).astype(F32)
        this = lax.broadcasted_iota(jnp.int32, (8, 1024), 0).astype(F32) + base
        found = jnp.sum(jnp.where(row == this, position, 0.0), axis=1, keepdims=True)
        label_column[1, pl.ds(pl.multiple_of(8 * n, 8), 8), :] = jnp.broadcast_to(found, (8, 128))
        return carry

    lax.fori_loop(0, 64, invert, 0)

    for which in chunks:
        core_copy(0, *which, 1 - c).wait_recv()

    @pl.when(other == 0)
    def _():
        for which in chunks:
            link_copy(5, *which).start()

    def inverse_norms(load):
        total = jnp.zeros((16, TILE), F32)
        for r in range(0, WIDTH, 16):
            part = load(r).astype(F32)
            total += part * part
        return lax.rsqrt(jnp.sum(total, axis=0, keepdims=True) + 1e-06)

    def normalise(load):
        inverse = inverse_norms(load)
        for r in range(0, WIDTH, 16):
            kn[r : r + 16, :] = (load(r).astype(F32) * inverse).astype(BF)

    for part in range(2):

        @pl.when(c == part)
        def _(part=part):
            mine[0] = text_a[0] if part == 0 else text_b[0]
            mine[1] = image_a[0] if part == 0 else image_b[0]

    def own_rows(array, carry):
        normalise(lambda r: mine[1 - array, r : r + 16, :])
        for b in range(0, WIDTH, 128):
            q[array, :, b : b + 128] = kn[b : b + 128, :].astype(F32).T.astype(BF)
        return carry

    lax.fori_loop(0, 2, own_rows, 0)
    acc[...] = jnp.zeros_like(acc)
    scale, bias = scale_in[0], bias_in[0]

    for_all = {
        2: [((2, 4), 0, 3)], 3: [((1, 3), 1, 0)], 4: [((2, 4), 1, 0)], 5: [((1, 3), 1, 1)], 7: [((2, 4), 1, 1), ((1, 3), 1, 2)],
        9: [((2, 4), 1, 2)], 10: [((1, 3), 1, 3)], 12: [((2, 4), 1, 3)],
    }
    z_near = {1: (0, 0), 3: (0, 1), 4: (0, 2), 5: (0, 3), 6: (1, 0), 7: (1, 1), 9: (1, 2), 10: (1, 3)}
    z_far = {3: (0, 0), 4: (0, 1), 5: (0, 2), 6: (0, 3), 8: (1, 0), 9: (1, 1), 11: (1, 2), 12: (1, 3)}

    def hand_over(step):
        for n in range(13):

            @pl.when(step == n)
            def _(n=n):
                if n in z_near:
                    pl.when(other == 1)(partial(pass_on, 5, *z_near[n]))
                if n in z_far:
                    pl.when(other == 0)(partial(pass_on, 6, *z_far[n]))
                for several, array, chunk in for_all.get(n, []):
                    for s in several:
                        pass_on(s, array, chunk)

    def finish(array):
        total = jnp.zeros((16, TILE), F32)
        for r in range(0, WIDTH, 16):
            total += mine[1 - array, r : r + 16, :].astype(F32) * acc[array, r : r + 16, :]
        inverse = inverse_norms(lambda r: mine[1 - array, r : r + 16, :])
        along = jnp.sum(total, axis=0, keepdims=True) * inverse * scale
        first, second = inverse * scale, inverse * inverse * along
        for r in range(0, WIDTH, 16):
            unit_part = mine[1 - array, r : r + 16, :].astype(F32) * second
            gradient_out[array, r : r + 16, :] = (first * acc[array, r : r + 16, :] - unit_part).astype(BF)

    def send(array):
        last_copy(array, 1 - a, home).start()

        @pl.when(other == 1)
        def _():
            last_copy(array, a, sibling).start()

        @pl.when(other == 0)
        def _():
            home_copy(array).start()

    def tile(step, carry):
        partnered = jnp.minimum(step // 4, 1)
        phase = (1 - partnered) * step + partnered * ((step - 4) // 3)
        array, part = phase // 2, phase % 2
        hand_over(step)
        value = table[(step + 2) % 3, 0]
        slot = sum(jnp.where(value == 1 << b, s, 0) for b, s in enumerate(SLOT_OF_BIT))
        for p in range(4):
            buffer = buffers[p // 2][p % 2]

            @pl.when(step == p)
            def _(buffer=buffer):
                normalise(lambda r: buffer[0, r : r + 16, :])

            @pl.when(step == 4 + 3 * p)
            def _(p=p):
                for s in range(1, 7):
                    for u in range(2):
                        core_copy(s, p // 2, 2 * (p % 2) + u, 1 - c).wait_recv()

            @pl.when((step >= 4 + 3 * p) & (step < 7 + 3 * p))
            def _(buffer=buffer):
                normalise(lambda r: buffer[slot, r : r + 16, :])

        logits = jnp.dot(q[array], kn[...], preferred_element_type=F32) * scale + bias
        weight = jax.nn.sigmoid(logits)
        shift = (TILE * part - 4096 * partnered).astype(F32)
        at = lax.broadcasted_iota(jnp.int32, (TILE, 128), 1).astype(F32) + shift
        column = label_column[array]
        positive = [jnp.where(column == at + 128.0 * u, 1.0, 0.0) for u in range(TILE // 128)]
        weight = (weight - jnp.concatenate(positive, axis=1)).astype(BF)
        acc[array] += lax.dot_general(kn[...], weight, NT, preferred_element_type=F32)

        @pl.when((step == 9) | (step == 15))
        def _():
            finish(array)

        pl.when(step == 9)(partial(send, 0))
        pl.when(step == 15)(partial(send, 1))
        return carry

    lax.fori_loop(0, 16, tile, 0)

    for array, chunk in chunks:
        for s in NEAR:
            link_copy(s, array, chunk).wait_send()
            relay_copy(s, array, chunk).wait_send()
        for s in range(7):
            core_copy(s, array, chunk, c).wait_send()

        @pl.when(other == 1)
        def _(array=array, chunk=chunk):
            swap_copy(array, chunk).wait_send()

    for array in range(2):
        for part in range(2):
            there = outputs[array].at[:, pl.ds(TILE * part, TILE)]
            here = (1 - other) * (1 - (part - c) * (part - c))

            @pl.when(here == 1)
            def _(array=array, part=part, there=there):
                pltpu.make_async_copy(gradient_out.at[array, columns_of(0), :], there, last_r.at[array, part]).wait()

            @pl.when(here == 0)
            def _(array=array, part=part, there=there):
                remote(
                    gradient_out.at[array, columns_of(0), :], there,
                    last_s.at[array, 0], last_r.at[array, part], across,
                ).wait_recv()

        last_copy(array, 1 - a, home).wait_send()

        @pl.when(other == 1)
        def _(array=array):
            last_copy(array, a, sibling).wait_send()


def per_device(image, text, scale, bias, table, labels):
    dma = pltpu.SemaphoreType.DMA
    smem, vmem = pl.BlockSpec(memory_space=pltpu.SMEM), pl.BlockSpec(memory_space=pltpu.VMEM)
    anywhere = pl.BlockSpec(memory_space=pl.ANY)
    text_grad, image_grad = pl.pallas_call(
        kernel,
        out_shape=[jax.ShapeDtypeStruct((DEPTH, ROWS), BF)] * 2,
        in_specs=[smem, smem, smem, vmem, anywhere, anywhere],
        out_specs=[anywhere] * 2,
        scratch_shapes=[pltpu.VMEM((7, WIDTH, TILE), BF)] * 4
        + [
            pltpu.VMEM((2, WIDTH, TILE), BF),
            pltpu.VMEM((2, TILE, WIDTH), BF),
            pltpu.VMEM((WIDTH, TILE), BF),
            pltpu.VMEM((2, WIDTH, TILE), F32),
            pltpu.VMEM((2, WIDTH, TILE), BF),
            pltpu.VMEM((1, ROWS), jnp.int32),
            pltpu.VMEM((2, TILE, 128), F32),
            dma((2, 4)), dma((2, 4)), dma((3, 2, 4)), dma((6, 2, 4)), dma((7, 2, 4)), dma((7, 2, 4)), dma((3, 2, 4)),
            dma((2, 2)), dma((2, 2)), dma, dma,
        ],
        compiler_params=pltpu.CompilerParams(collective_id=0, has_side_effects=True, vmem_limit_bytes=58 * 2**20),
        cost_estimate=pl.CostEstimate(flops=20 * 10**9, bytes_accessed=6 * 10**6, transcendentals=4 * 2**20),
        name="rounds",
    )(table, scale.reshape(1), bias.reshape(1), labels, text.T, image.T)
    return image_grad.T.astype(F32), text_grad.T.astype(F32)


def solution(mesh):
    return jax.shard_map(
        per_device,
        mesh=mesh,
        in_specs=(P("dp", "tower"), P("dp", "tower"), P(), P(), P(), P("dp", None)),
        out_specs=(P("dp", "tower"), P("dp", "tower")),
        check_vma=False,
    )
```

time: 663 us -> 126 us (0.19)
  waiting for transfers between devices: 549 us -> 0 us
  Pallas kernels: 0 us -> 120 us
  matrix products: 47.9 us -> 0 us
  between operations: 25 us -> 1.93 us
  other arithmetic: 16.7 us -> 4.34 us
  starting transfers between devices: 11.1 us -> 0 us
  blocking collectives: 8.66 us -> 0 us
    psum x1 -> x0, waiting for transfers between devices: 389 us -> none  [summed_tile(): return lax.psum(tile, 'tower')]
    ppermute x6 -> x0, waiting for transfers between devices: 161 us -> none  [from_partner_2(): lax.ppermute(array, axis, [(i, i ^ 1 << distance) for i in range(lax.axis...]
    pallas_call x0 -> x1, Pallas kernels: none -> 120 us  [per_device(): pl.pallas_call(kernel, out_shape=[jax.ShapeDtypeStruct((DEPTH, ROWS), BF)...]
    dot_general x12 -> x0, matrix products: 47.9 us -> none  [the longest x4 19.1 us: similarity(): jnp.dot(normed_image, text_half.T, preferred_element_type=jnp.float32)]
    ppermute x6 -> x0, starting transfers between devices: 11.1 us -> none  [from_partner_2(): lax.ppermute(array, axis, [(i, i ^ 1 << distance) for i in range(lax.axis...]
    psum x2 -> x0, blocking collectives: 8.66 us -> none  [the longest x1 4.84 us: per_device(): lax.psum((jnp.sum(wide_image * wide_image, axis=1), jnp.sum(wide_text * w...]
  transfers between devices with their start and end apart: 7 -> 0, of which waited for: 7 -> 0; matrix products, arithmetic and copies ran while one was open for 0% -> 0% of each run, Pallas kernels for 0% -> 0%
where the time goes in v1:
time: 126 us
  Pallas kernels  120 us (95%)
  other arithmetic  4.34 us (3%)
  between operations  1.93 us (2%)
    pallas_call x1, Pallas kernels, per_device(): pl.pallas_call(kernel, out_shape=[jax.ShapeDtypeStruct((DEPTH, ROWS), BF)...  120 us
    convert_element_type x1, other arithmetic, per_device(): return (image_grad.T.astype(F32), text_grad.T.astype(F32))  4.34 us

profile of v1, /device:TPU:1, one launch (start us, length us, event | category | flops | bytes accessed | tf_op | source)
XLA Modules:
  0.0 125.9 jit_solution(16393555091688767465)
XLA Ops:
  1.9 119.6 %rounds.1 = (bf16[576,1024]{1,0:T(8,128)(2,1)}, bf16[576,1024]{1,0:T(8,128)(2,1)}) custom-call(s32[3,64]{1,0:T(4,128)} %table.1, f32[1]{0:T(128)} %bitcast.8.scale_in, f32[1]{0:T(128)} %bitcast.9.bias_in, s32[1,1024]{1,0:T(1,128)} %labels_in.1, bf16[576,1024]{1,0:T(8,128)(2,1)} %bitcast.10, bf16[576,1024]{1,0:T(8,128)(2,1)} %bitcast.11), custom_call_target="tpu_custom_call" | custom-call | flops 20000000000 | bytes 6000000 | tf_op jit(solution)/shard_map/rounds/pallas_call | solution.py:352
  121.6 4.3 %convert_bitcast_fusion = (f32[1024,576]{0,1:T(8,128)}, f32[1024,576]{0,1:T(8,128)}) fusion(bf16[576,1024]{1,0:T(8,128)(2,1)} %get-tuple-element.5, bf16[576,1024]{1,0:T(8,128)(2,1)} %get-tuple-element.4), kind=kLoop, calls=%fused_computation | loop fusion | flops 1179648 | bytes 7077888 | tf_op jit(solution)/shard_map/convert_element_type | solution.py:373

commit v2 on v1

--- a/solution.py
+++ b/solution.py
@@ -15,6 +15,7 @@
 CHUNK, TILE = 256, 512
 SLOT_OF_BIT = (5, 1, 2, 6, 3, 4)
 NEAR = (1, 3, 5)
+GATE = 5
 
 
 def flip(index, bit):
@@ -131,9 +132,9 @@
     def pass_text(chunk):
         for s in (1, 3):
             pass_on(s, 0, chunk)
-        if chunk > 0:
+        if chunk > 1:
             for s in (2, 4):
-                pass_on(s, 0, chunk - 1)
+                pass_on(s, 0, chunk - 2)
 
     chunks = [(array, chunk) for array in range(2) for chunk in range(4)]
     label_copy = remote(labels_in, labels, label_s, label_r, sibling)
@@ -147,15 +148,11 @@
 
     @pl.when(other == 0)
     def _():
+        label_copy.start()
+        labels[...] = labels_in[...]
         for which in chunks:
             own_copy(*which).wait()
             fan_out(*which)
-        label_copy.start()
-        labels[...] = labels_in[...]
-        for which in chunks:
-            pass_on(5, *which)
-        for chunk in range(4):
-            pass_text(chunk)
         label_copy.wait_send()
 
     @pl.when(other == 1)
@@ -164,14 +161,6 @@
             swap_copy(*which).start()
         for which in chunks:
             beside_copy(*which).start()
-        for n, which in enumerate(chunks):
-            swap_wait(*which)
-            fan_out(*which)
-            if n > 0:
-                pass_on(6, *chunks[n - 1])
-            if n % 2 == 1:
-                pass_text(n // 2)
-        pass_on(6, *chunks[7])
         label_copy.wait_recv()
 
     for b in range(4):
@@ -189,13 +178,23 @@
 
     lax.fori_loop(0, 64, invert, 0)
 
-    for which in chunks:
-        core_copy(0, *which, 1 - c).wait_recv()
+    def swapped_in(first, last):
+        for n in range(first, last):
+            swap_wait(*chunks[n])
+            fan_out(*chunks[n])
+            if n > 1:
+                pass_on(6, *chunks[n - 2])
+            if n % 2 == 1:
+                pass_text(n // 2)
 
     @pl.when(other == 0)
     def _():
         for which in chunks:
-            link_copy(5, *which).start()
+            pass_on(5, *which)
+        pass_text(0)
+        pass_text(1)
+
+    pl.when(other == 1)(partial(swapped_in, 0, 5))
 
     def inverse_norms(load):
         total = jnp.zeros((16, TILE), F32)
@@ -209,42 +208,72 @@
         for r in range(0, WIDTH, 16):
             kn[r : r + 16, :] = (load(r).astype(F32) * inverse).astype(BF)
 
-    for part in range(2):
-
-        @pl.when(c == part)
-        def _(part=part):
-            mine[0] = text_a[0] if part == 0 else text_b[0]
-            mine[1] = image_a[0] if part == 0 else image_b[0]
-
-    def own_rows(array, carry):
-        normalise(lambda r: mine[1 - array, r : r + 16, :])
+    def own_rows(array):
+        for part in range(2):
+
+            @pl.when(c == part)
+            def _(part=part):
+                mine[array] = buffers[array][part][0]
+
+        normalise(lambda r: mine[array, r : r + 16, :])
         for b in range(0, WIDTH, 128):
-            q[array, :, b : b + 128] = kn[b : b + 128, :].astype(F32).T.astype(BF)
-        return carry
-
-    lax.fori_loop(0, 2, own_rows, 0)
+            q[1 - array, :, b : b + 128] = kn[b : b + 128, :].astype(F32).T.astype(BF)
+
+    for chunk in range(4):
+        core_copy(0, 0, chunk, 1 - c).wait_recv()
+    own_rows(0)
+
+    @pl.when(other == 0)
+    def _():
+        pass_text(2)
+        for n in range(4, 8):
+            if n <= GATE:
+                core_copy(0, *chunks[n], 1 - c).wait_recv()
+        for first in chunks[: 7 - GATE]:
+            link_copy(5, *first).start()
+        for n in range(GATE + 1, 8):
+            core_copy(0, *chunks[n], 1 - c).wait_recv()
+        for which in chunks[7 - GATE :]:
+            link_copy(5, *which).start()
+        pass_text(3)
+
+    @pl.when(other == 1)
+    def _():
+        swapped_in(5, 8)
+        pass_on(6, *chunks[6])
+        pass_on(6, *chunks[7])
+        for n in range(4, 8):
+            core_copy(0, *chunks[n], 1 - c).wait_recv()
+
+    own_rows(1)
     acc[...] = jnp.zeros_like(acc)
     scale, bias = scale_in[0], bias_in[0]
 
-    for_all = {
-        2: [((2, 4), 0, 3)], 3: [((1, 3), 1, 0)], 4: [((2, 4), 1, 0)], 5: [((1, 3), 1, 1)], 7: [((2, 4), 1, 1), ((1, 3), 1, 2)],
-        9: [((2, 4), 1, 2)], 10: [((1, 3), 1, 3)], 12: [((2, 4), 1, 3)],
+    plan = {
+        0: [((2, 4), 0, 2)],
+        1: [((5,), 0, 0)],
+        2: [((1, 3), 1, 0)],
+        3: [((5,), 0, 1), ((2, 4), 0, 3), ((6,), 0, 0)],
+        4: [((5,), 0, 2), ((6,), 0, 1), ((1, 3), 1, 1), ((5,), 0, 3)],
+        5: [((2, 4), 1, 0), ((6,), 0, 2)],
+        6: [((5,), 1, 0)],
+        7: [((6,), 0, 3), ((1, 3), 1, 2)],
+        8: [((5,), 1, 1), ((2, 4), 1, 1), ((6,), 1, 0)],
+        9: [((5,), 1, 2)],
+        10: [((6,), 1, 1), ((1, 3), 1, 3), ((5,), 1, 3)],
+        11: [((2, 4), 1, 2), ((6,), 1, 2)],
+        13: [((6,), 1, 3), ((2, 4), 1, 3)],
     }
-    z_near = {1: (0, 0), 3: (0, 1), 4: (0, 2), 5: (0, 3), 6: (1, 0), 7: (1, 1), 9: (1, 2), 10: (1, 3)}
-    z_far = {3: (0, 0), 4: (0, 1), 5: (0, 2), 6: (0, 3), 8: (1, 0), 9: (1, 1), 11: (1, 2), 12: (1, 3)}
-
-    def hand_over(step):
-        for n in range(13):
-
-            @pl.when(step == n)
-            def _(n=n):
-                if n in z_near:
-                    pl.when(other == 1)(partial(pass_on, 5, *z_near[n]))
-                if n in z_far:
-                    pl.when(other == 0)(partial(pass_on, 6, *z_far[n]))
-                for several, array, chunk in for_all.get(n, []):
-                    for s in several:
-                        pass_on(s, array, chunk)
+
+    def hand_over(n):
+        for several, array, chunk in plan.get(n, []):
+            for s in several:
+                if s == 5:
+                    pl.when(other == 1)(partial(pass_on, s, array, chunk))
+                elif s == 6:
+                    pl.when(other == 0)(partial(pass_on, s, array, chunk))
+                else:
+                    pass_on(s, array, chunk)
 
     def finish(array):
         total = jnp.zeros((16, TILE), F32)
@@ -268,48 +297,42 @@
         def _():
             home_copy(array).start()
 
-    def tile(step, carry):
-        partnered = jnp.minimum(step // 4, 1)
-        phase = (1 - partnered) * step + partnered * ((step - 4) // 3)
-        array, part = phase // 2, phase % 2
-        hand_over(step)
-        value = table[(step + 2) % 3, 0]
-        slot = sum(jnp.where(value == 1 << b, s, 0) for b, s in enumerate(SLOT_OF_BIT))
-        for p in range(4):
-            buffer = buffers[p // 2][p % 2]
-
-            @pl.when(step == p)
-            def _(buffer=buffer):
-                normalise(lambda r: buffer[0, r : r + 16, :])
-
-            @pl.when(step == 4 + 3 * p)
-            def _(p=p):
-                for s in range(1, 7):
-                    for u in range(2):
-                        core_copy(s, p // 2, 2 * (p % 2) + u, 1 - c).wait_recv()
-
-            @pl.when((step >= 4 + 3 * p) & (step < 7 + 3 * p))
-            def _(buffer=buffer):
-                normalise(lambda r: buffer[slot, r : r + 16, :])
-
+    def tile(load, array, part, own):
+        normalise(load)
         logits = jnp.dot(q[array], kn[...], preferred_element_type=F32) * scale + bias
         weight = jax.nn.sigmoid(logits)
-        shift = (TILE * part - 4096 * partnered).astype(F32)
-        at = lax.broadcasted_iota(jnp.int32, (TILE, 128), 1).astype(F32) + shift
-        column = label_column[array]
-        positive = [jnp.where(column == at + 128.0 * u, 1.0, 0.0) for u in range(TILE // 128)]
-        weight = (weight - jnp.concatenate(positive, axis=1)).astype(BF)
-        acc[array] += lax.dot_general(kn[...], weight, NT, preferred_element_type=F32)
-
-        @pl.when((step == 9) | (step == 15))
-        def _():
+        if own:
+            at = lax.broadcasted_iota(jnp.int32, (TILE, 128), 1).astype(F32) + float(TILE * part)
+            column = label_column[array]
+            positive = [jnp.where(column == at + 128.0 * u, 1.0, 0.0) for u in range(TILE // 128)]
+            weight = weight - jnp.concatenate(positive, axis=1)
+        acc[array] += lax.dot_general(kn[...], weight.astype(BF), NT, preferred_element_type=F32)
+
+    for n in range(4):
+        array, part = n // 2, n % 2
+        hand_over(n)
+        tile(lambda r, buffer=buffers[array][part]: buffer[0, r : r + 16, :], array, part, True)
+
+    for n in range(4):
+        array, part = n // 2, n % 2
+        buffer = buffers[array][part]
+        hand_over(4 + 3 * n)
+        for s in range(1, 7):
+            for u in range(2):
+                core_copy(s, array, 2 * part + u, 1 - c).wait_recv()
+
+        def partner_tile(k, carry, n=n, array=array, part=part, buffer=buffer):
+            for later in (1, 2):
+                pl.when(k == later)(partial(hand_over, 4 + 3 * n + later))
+            value = table[k, 0]
+            slot = sum(jnp.where(value == 1 << b, s, 0) for b, s in enumerate(SLOT_OF_BIT))
+            tile(lambda r: buffer[slot, r : r + 16, :], array, part, False)
+            return carry
+
+        lax.fori_loop(0, 3, partner_tile, 0)
+        if part == 1:
             finish(array)
-
-        pl.when(step == 9)(partial(send, 0))
-        pl.when(step == 15)(partial(send, 1))
-        return carry
-
-    lax.fori_loop(0, 16, tile, 0)
+            send(array)
 
     for array, chunk in chunks:
         for s in NEAR:

time: 126 us -> 108 us (0.86)
  Pallas kernels: 120 us -> 102 us
    pallas_call x1, Pallas kernels: 120 us -> 102 us  [per_device(): pl.pallas_call(kernel, out_shape=[jax.ShapeDtypeStruct((DEPTH, ROWS), BF)...]
where the time goes in v2:
time: 108 us
  Pallas kernels  102 us (94%)
  other arithmetic  4.34 us (4%)
  between operations  1.93 us (2%)
    pallas_call x1, Pallas kernels, per_device(): pl.pallas_call(kernel, out_shape=[jax.ShapeDtypeStruct((DEPTH, ROWS), BF)...  102 us
    convert_element_type x1, other arithmetic, per_device(): return (image_grad.T.astype(F32), text_grad.T.astype(F32))  4.34 us

profile of v2, /device:TPU:1, one launch (start us, length us, event | category | flops | bytes accessed | tf_op | source)
XLA Modules:
  0.0 108.1 jit_solution(7147456716458127658)
XLA Ops:
  1.9 101.8 %rounds.1 = (bf16[576,1024]{1,0:T(8,128)(2,1)}, bf16[576,1024]{1,0:T(8,128)(2,1)}) custom-call(s32[3,64]{1,0:T(4,128)} %table.1, f32[1]{0:T(128)} %bitcast.8.scale_in, f32[1]{0:T(128)} %bitcast.9.bias_in, s32[1,1024]{1,0:T(1,128)} %labels_in.1, bf16[576,1024]{1,0:T(8,128)(2,1)} %bitcast.10, bf16[576,1024]{1,0:T(8,128)(2,1)} %bitcast.11), custom_call_target="tpu_custom_call" | custom-call | flops 20000000000 | bytes 6000000 | tf_op jit(solution)/shard_map/rounds/pallas_call | solution.py:375
  103.8 4.3 %convert_bitcast_fusion = (f32[1024,576]{0,1:T(8,128)}, f32[1024,576]{0,1:T(8,128)}) fusion(bf16[576,1024]{1,0:T(8,128)(2,1)} %get-tuple-element.5, bf16[576,1024]{1,0:T(8,128)(2,1)} %get-tuple-element.4), kind=kLoop, calls=%fused_computation | loop fusion | flops 1179648 | bytes 7077888 | tf_op jit(solution)/shard_map/convert_element_type | solution.py:396

commit v3 on v2

--- a/solution.py
+++ b/solution.py
@@ -101,19 +101,21 @@
             core_s.at[s, array, chunk], core_r.at[s, array, chunk], sibling,
         )
 
-    def last_copy(array, half, device):
-        return remote(
-            gradient_out.at[array, columns_of(half), :],
-            outputs[array].at[:, pl.ds(pl.multiple_of(TILE * c, TILE), TILE)],
-            last_s.at[array, half], last_r.at[array, c], device,
-        )
-
-    def home_copy(array):
-        return pltpu.make_async_copy(
-            gradient_out.at[array, columns_of(a), :],
-            outputs[array].at[:, pl.ds(pl.multiple_of(TILE * c, TILE), TILE)],
-            last_r.at[array, c],
-        )
+    def result(array, half, piece):
+        return gradient_out.at[array, columns_of(half), rows_of(piece)]
+
+    def landing(array, piece):
+        row = pl.multiple_of(TILE * c + CHUNK * piece, CHUNK)
+        return outputs[array].at[:, pl.ds(row, CHUNK)]
+
+    def last_copy(array, half, piece, device):
+        return remote(
+            result(array, half, piece), landing(array, piece),
+            last_s.at[array, half, piece], last_r.at[array, c, piece], device,
+        )
+
+    def home_copy(array, piece):
+        return pltpu.make_async_copy(result(array, a, piece), landing(array, piece), last_r.at[array, c, piece])
 
     def pass_on(s, array, chunk):
         remote(
@@ -203,10 +205,10 @@
             total += part * part
         return lax.rsqrt(jnp.sum(total, axis=0, keepdims=True) + 1e-06)
 
-    def normalise(load):
+    def normalise(load, k=0):
         inverse = inverse_norms(load)
         for r in range(0, WIDTH, 16):
-            kn[r : r + 16, :] = (load(r).astype(F32) * inverse).astype(BF)
+            kn[k, r : r + 16, :] = (load(r).astype(F32) * inverse).astype(BF)
 
     def own_rows(array):
         for part in range(2):
@@ -217,7 +219,7 @@
 
         normalise(lambda r: mine[array, r : r + 16, :])
         for b in range(0, WIDTH, 128):
-            q[1 - array, :, b : b + 128] = kn[b : b + 128, :].astype(F32).T.astype(BF)
+            q[1 - array, :, b : b + 128] = kn[0, b : b + 128, :].astype(F32).T.astype(BF)
 
     for chunk in range(4):
         core_copy(0, 0, chunk, 1 - c).wait_recv()
@@ -275,43 +277,50 @@
                 else:
                     pass_on(s, array, chunk)
 
-    def finish(array):
-        total = jnp.zeros((16, TILE), F32)
+    def finish(array, piece):
+        rows = rows_of(piece)
+        total = jnp.zeros((16, CHUNK), F32)
+        square = jnp.zeros((16, CHUNK), F32)
         for r in range(0, WIDTH, 16):
-            total += mine[1 - array, r : r + 16, :].astype(F32) * acc[array, r : r + 16, :]
-        inverse = inverse_norms(lambda r: mine[1 - array, r : r + 16, :])
+            own = mine[1 - array, r : r + 16, rows].astype(F32)
+            square += own * own
+            total += own * acc[array, r : r + 16, rows]
+        inverse = lax.rsqrt(jnp.sum(square, axis=0, keepdims=True) + 1e-06)
         along = jnp.sum(total, axis=0, keepdims=True) * inverse * scale
         first, second = inverse * scale, inverse * inverse * along
         for r in range(0, WIDTH, 16):
-            unit_part = mine[1 - array, r : r + 16, :].astype(F32) * second
-            gradient_out[array, r : r + 16, :] = (first * acc[array, r : r + 16, :] - unit_part).astype(BF)
-
-    def send(array):
-        last_copy(array, 1 - a, home).start()
+            unit_part = mine[1 - array, r : r + 16, rows].astype(F32) * second
+            gradient_out[array, r : r + 16, rows] = (first * acc[array, r : r + 16, rows] - unit_part).astype(BF)
+        last_copy(array, 1 - a, piece, home).start()
 
         @pl.when(other == 1)
         def _():
-            last_copy(array, a, sibling).start()
+            last_copy(array, a, piece, sibling).start()
 
         @pl.when(other == 0)
         def _():
-            home_copy(array).start()
-
-    def tile(load, array, part, own):
-        normalise(load)
-        logits = jnp.dot(q[array], kn[...], preferred_element_type=F32) * scale + bias
+            home_copy(array, piece).start()
+
+    def tile(array, part, own, k=0, first=0, size=TILE):
+        rows = pl.ds(first, size)
+        logits = jnp.dot(q[array, rows, :], kn[k], preferred_element_type=F32) * scale + bias
         weight = jax.nn.sigmoid(logits)
         if own:
             at = lax.broadcasted_iota(jnp.int32, (TILE, 128), 1).astype(F32) + float(TILE * part)
             column = label_column[array]
             positive = [jnp.where(column == at + 128.0 * u, 1.0, 0.0) for u in range(TILE // 128)]
             weight = weight - jnp.concatenate(positive, axis=1)
-        acc[array] += lax.dot_general(kn[...], weight.astype(BF), NT, preferred_element_type=F32)
+        acc[array, :, rows] += lax.dot_general(kn[k], weight.astype(BF), NT, preferred_element_type=F32)
+
+    def slot_of(k):
+        value = table[k, 0]
+        return sum(jnp.where(value == 1 << b, s, 0) for b, s in enumerate(SLOT_OF_BIT))
 
     for n in range(4):
         array, part = n // 2, n % 2
         hand_over(n)
-        tile(lambda r, buffer=buffers[array][part]: buffer[0, r : r + 16, :], array, part, True)
+        normalise(lambda r, buffer=buffers[array][part]: buffer[0, r : r + 16, :])
+        tile(array, part, True)
 
     for n in range(4):
         array, part = n // 2, n % 2
@@ -321,18 +330,29 @@
             for u in range(2):
                 core_copy(s, array, 2 * part + u, 1 - c).wait_recv()
 
+        if n == 3:
+            for k in range(3):
+                slot = slot_of(k)
+                normalise(lambda r, slot=slot, buffer=buffer: buffer[slot, r : r + 16, :], k)
+                tile(array, part, False, k, 0, CHUNK)
+            finish(array, 0)
+            for k in range(3):
+                tile(array, part, False, k, CHUNK, CHUNK)
+            finish(array, 1)
+            continue
+
         def partner_tile(k, carry, n=n, array=array, part=part, buffer=buffer):
             for later in (1, 2):
                 pl.when(k == later)(partial(hand_over, 4 + 3 * n + later))
-            value = table[k, 0]
-            slot = sum(jnp.where(value == 1 << b, s, 0) for b, s in enumerate(SLOT_OF_BIT))
-            tile(lambda r: buffer[slot, r : r + 16, :], array, part, False)
+            slot = slot_of(k)
+            normalise(lambda r: buffer[slot, r : r + 16, :])
+            tile(array, part, False)
             return carry
 
         lax.fori_loop(0, 3, partner_tile, 0)
-        if part == 1:
-            finish(array)
-            send(array)
+        if n == 1:
+            finish(array, 0)
+            finish(array, 1)
 
     for array, chunk in chunks:
         for s in NEAR:
@@ -346,26 +366,26 @@
             swap_copy(array, chunk).wait_send()
 
     for array in range(2):
-        for part in range(2):
-            there = outputs[array].at[:, pl.ds(TILE * part, TILE)]
-            here = (1 - other) * (1 - (part - c) * (part - c))
-
-            @pl.when(here == 1)
-            def _(array=array, part=part, there=there):
-                pltpu.make_async_copy(gradient_out.at[array, columns_of(0), :], there, last_r.at[array, part]).wait()
-
-            @pl.when(here == 0)
-            def _(array=array, part=part, there=there):
-                remote(
-                    gradient_out.at[array, columns_of(0), :], there,
-                    last_s.at[array, 0], last_r.at[array, part], across,
-                ).wait_recv()
-
-        last_copy(array, 1 - a, home).wait_send()
-
-        @pl.when(other == 1)
-        def _(array=array):
-            last_copy(array, a, sibling).wait_send()
+        for piece in range(2):
+            for part in range(2):
+                there = outputs[array].at[:, rows_of(2 * part + piece)]
+                here = (1 - other) * (1 - (part - c) * (part - c))
+
+                @pl.when(here == 1)
+                def _(array=array, part=part, piece=piece, there=there):
+                    pltpu.make_async_copy(result(array, 0, piece), there, last_r.at[array, part, piece]).wait()
+
+                @pl.when(here == 0)
+                def _(array=array, part=part, piece=piece, there=there):
+                    remote(
+                        result(array, 0, piece), there, last_s.at[array, 0, piece], last_r.at[array, part, piece], across
+                    ).wait_recv()
+
+            last_copy(array, 1 - a, piece, home).wait_send()
+
+            @pl.when(other == 1)
+            def _(array=array, piece=piece):
+                last_copy(array, a, piece, sibling).wait_send()
 
 
 def per_device(image, text, scale, bias, table, labels):
@@ -381,13 +401,13 @@
         + [
             pltpu.VMEM((2, WIDTH, TILE), BF),
             pltpu.VMEM((2, TILE, WIDTH), BF),
-            pltpu.VMEM((WIDTH, TILE), BF),
+            pltpu.VMEM((3, WIDTH, TILE), BF),
             pltpu.VMEM((2, WIDTH, TILE), F32),
             pltpu.VMEM((2, WIDTH, TILE), BF),
             pltpu.VMEM((1, ROWS), jnp.int32),
             pltpu.VMEM((2, TILE, 128), F32),
             dma((2, 4)), dma((2, 4)), dma((3, 2, 4)), dma((6, 2, 4)), dma((7, 2, 4)), dma((7, 2, 4)), dma((3, 2, 4)),
-            dma((2, 2)), dma((2, 2)), dma, dma,
+            dma((2, 2, 2)), dma((2, 2, 2)), dma, dma,
         ],
         compiler_params=pltpu.CompilerParams(collective_id=0, has_side_effects=True, vmem_limit_bytes=58 * 2**20),
         cost_estimate=pl.CostEstimate(flops=20 * 10**9, bytes_accessed=6 * 10**6, transcendentals=4 * 2**20),

time: 108 us -> 106 us (0.981)
  Pallas kernels: 102 us -> 99.7 us
    pallas_call x1, Pallas kernels: 102 us -> 99.7 us  [per_device(): pl.pallas_call(kernel, out_shape=[jax.ShapeDtypeStruct((DEPTH, ROWS), BF)...]
where the time goes in v3:
time: 106 us
  Pallas kernels  99.7 us (94%)
  other arithmetic  4.34 us (4%)
  between operations  1.93 us (2%)
    pallas_call x1, Pallas kernels, per_device(): pl.pallas_call(kernel, out_shape=[jax.ShapeDtypeStruct((DEPTH, ROWS), BF)...  99.7 us
    convert_element_type x1, other arithmetic, per_device(): return (image_grad.T.astype(F32), text_grad.T.astype(F32))  4.34 us

profile of v3, /device:TPU:1, one launch (start us, length us, event | category | flops | bytes accessed | tf_op | source)
XLA Modules:
  0.0 106.0 jit_solution(5613632117523684354)
XLA Ops:
  1.9 99.7 %rounds.1 = (bf16[576,1024]{1,0:T(8,128)(2,1)}, bf16[576,1024]{1,0:T(8,128)(2,1)}) custom-call(s32[3,64]{1,0:T(4,128)} %table.1, f32[1]{0:T(128)} %bitcast.8.scale_in, f32[1]{0:T(128)} %bitcast.9.bias_in, s32[1,1024]{1,0:T(1,128)} %labels_in.1, bf16[576,1024]{1,0:T(8,128)(2,1)} %bitcast.10, bf16[576,1024]{1,0:T(8,128)(2,1)} %bitcast.11), custom_call_target="tpu_custom_call" | custom-call | flops 20000000000 | bytes 6000000 | tf_op jit(solution)/shard_map/rounds/pallas_call | solution.py:395
  101.7 4.3 %convert_bitcast_fusion = (f32[1024,576]{0,1:T(8,128)}, f32[1024,576]{0,1:T(8,128)}) fusion(bf16[576,1024]{1,0:T(8,128)(2,1)} %get-tuple-element.5, bf16[576,1024]{1,0:T(8,128)(2,1)} %get-tuple-element.4), kind=kLoop, calls=%fused_computation | loop fusion | flops 1179648 | bytes 7077888 | tf_op jit(solution)/shard_map/convert_element_type | solution.py:416

commit v4 on v3

--- a/solution.py
+++ b/solution.py
@@ -253,16 +253,16 @@
 
     plan = {
         0: [((2, 4), 0, 2)],
-        1: [((5,), 0, 0)],
-        2: [((1, 3), 1, 0)],
-        3: [((5,), 0, 1), ((2, 4), 0, 3), ((6,), 0, 0)],
-        4: [((5,), 0, 2), ((6,), 0, 1), ((1, 3), 1, 1), ((5,), 0, 3)],
-        5: [((2, 4), 1, 0), ((6,), 0, 2)],
-        6: [((5,), 1, 0)],
-        7: [((6,), 0, 3), ((1, 3), 1, 2)],
-        8: [((5,), 1, 1), ((2, 4), 1, 1), ((6,), 1, 0)],
-        9: [((5,), 1, 2)],
-        10: [((6,), 1, 1), ((1, 3), 1, 3), ((5,), 1, 3)],
+        1: [((5,), 0, 0), ((1, 3), 1, 0)],
+        2: [((5,), 0, 1)],
+        3: [((2, 4), 0, 3), ((5,), 0, 2), ((6,), 0, 0)],
+        4: [((1, 3), 1, 1), ((5,), 0, 3), ((6,), 0, 1)],
+        5: [((5,), 1, 0), ((2, 4), 1, 0), ((6,), 0, 2)],
+        6: [((1, 3), 1, 2)],
+        7: [((5,), 1, 1), ((6,), 0, 3)],
+        8: [((5,), 1, 2), ((2, 4), 1, 1)],
+        9: [((1, 3), 1, 3), ((6,), 1, 0)],
+        10: [((5,), 1, 3), ((6,), 1, 1)],
         11: [((2, 4), 1, 2), ((6,), 1, 2)],
         13: [((6,), 1, 3), ((2, 4), 1, 3)],
     }

time: 106 us -> 103 us (0.972)
  Pallas kernels: 99.7 us -> 96.6 us
    pallas_call x1, Pallas kernels: 99.7 us -> 96.6 us  [per_device(): pl.pallas_call(kernel, out_shape=[jax.ShapeDtypeStruct((DEPTH, ROWS), BF)...]
where the time goes in v4:
time: 103 us
  Pallas kernels  96.6 us (94%)
  other arithmetic  4.34 us (4%)
  between operations  1.93 us (2%)
    pallas_call x1, Pallas kernels, per_device(): pl.pallas_call(kernel, out_shape=[jax.ShapeDtypeStruct((DEPTH, ROWS), BF)...  96.6 us
    convert_element_type x1, other arithmetic, per_device(): return (image_grad.T.astype(F32), text_grad.T.astype(F32))  4.34 us

profile of v4, /device:TPU:1, one launch (start us, length us, event | category | flops | bytes accessed | tf_op | source)
XLA Modules:
  0.0 102.9 jit_solution(4057355979380665629)
XLA Ops:
  1.9 96.6 %rounds.1 = (bf16[576,1024]{1,0:T(8,128)(2,1)}, bf16[576,1024]{1,0:T(8,128)(2,1)}) custom-call(s32[3,64]{1,0:T(4,128)} %table.1, f32[1]{0:T(128)} %bitcast.8.scale_in, f32[1]{0:T(128)} %bitcast.9.bias_in, s32[1,1024]{1,0:T(1,128)} %labels_in.1, bf16[576,1024]{1,0:T(8,128)(2,1)} %bitcast.10, bf16[576,1024]{1,0:T(8,128)(2,1)} %bitcast.11), custom_call_target="tpu_custom_call" | custom-call | flops 20000000000 | bytes 6000000 | tf_op jit(solution)/shard_map/rounds/pallas_call | solution.py:395
  98.6 4.3 %convert_bitcast_fusion = (f32[1024,576]{0,1:T(8,128)}, f32[1024,576]{0,1:T(8,128)}) fusion(bf16[576,1024]{1,0:T(8,128)(2,1)} %get-tuple-element.5, bf16[576,1024]{1,0:T(8,128)(2,1)} %get-tuple-element.4), kind=kLoop, calls=%fused_computation | loop fusion | flops 1179648 | bytes 7077888 | tf_op jit(solution)/shard_map/convert_element_type | solution.py:416

commit v5 on v4

--- a/solution.py
+++ b/solution.py
@@ -255,14 +255,14 @@
         0: [((2, 4), 0, 2)],
         1: [((5,), 0, 0), ((1, 3), 1, 0)],
         2: [((5,), 0, 1)],
-        3: [((2, 4), 0, 3), ((5,), 0, 2), ((6,), 0, 0)],
-        4: [((1, 3), 1, 1), ((5,), 0, 3), ((6,), 0, 1)],
-        5: [((5,), 1, 0), ((2, 4), 1, 0), ((6,), 0, 2)],
-        6: [((1, 3), 1, 2)],
-        7: [((5,), 1, 1), ((6,), 0, 3)],
+        3: [((5,), 0, 2), ((2, 4), 0, 3), ((6,), 0, 0)],
+        4: [((1, 3), 1, 1), ((5,), 0, 3), ((6,), 0, 1), ((5,), 1, 0)],
+        5: [((2, 4), 1, 0), ((6,), 0, 2)],
+        6: [((1, 3), 1, 2), ((5,), 1, 1)],
+        7: [((6,), 0, 3)],
         8: [((5,), 1, 2), ((2, 4), 1, 1)],
-        9: [((1, 3), 1, 3), ((6,), 1, 0)],
-        10: [((5,), 1, 3), ((6,), 1, 1)],
+        9: [((1, 3), 1, 3), ((5,), 1, 3), ((6,), 1, 0)],
+        10: [((6,), 1, 1)],
         11: [((2, 4), 1, 2), ((6,), 1, 2)],
         13: [((6,), 1, 3), ((2, 4), 1, 3)],
     }

time: 103 us -> 103 us (level)
  no operation moved by 1% of the time
where the time goes in v5:
time: 103 us
  Pallas kernels  96.5 us (94%)
  other arithmetic  4.34 us (4%)
  between operations  1.93 us (2%)
    pallas_call x1, Pallas kernels, per_device(): pl.pallas_call(kernel, out_shape=[jax.ShapeDtypeStruct((DEPTH, ROWS), BF)...  96.5 us
    convert_element_type x1, other arithmetic, per_device(): return (image_grad.T.astype(F32), text_grad.T.astype(F32))  4.34 us

profile of v5, /device:TPU:1, one launch (start us, length us, event | category | flops | bytes accessed | tf_op | source)
XLA Modules:
  0.0 102.8 jit_solution(14311903007484877721)
XLA Ops:
  1.9 96.5 %rounds.1 = (bf16[576,1024]{1,0:T(8,128)(2,1)}, bf16[576,1024]{1,0:T(8,128)(2,1)}) custom-call(s32[3,64]{1,0:T(4,128)} %table.1, f32[1]{0:T(128)} %bitcast.8.scale_in, f32[1]{0:T(128)} %bitcast.9.bias_in, s32[1,1024]{1,0:T(1,128)} %labels_in.1, bf16[576,1024]{1,0:T(8,128)(2,1)} %bitcast.10, bf16[576,1024]{1,0:T(8,128)(2,1)} %bitcast.11), custom_call_target="tpu_custom_call" | custom-call | flops 20000000000 | bytes 6000000 | tf_op jit(solution)/shard_map/rounds/pallas_call | solution.py:395
  98.5 4.3 %convert_bitcast_fusion = (f32[1024,576]{0,1:T(8,128)}, f32[1024,576]{0,1:T(8,128)}) fusion(bf16[576,1024]{1,0:T(8,128)(2,1)} %get-tuple-element.5, bf16[576,1024]{1,0:T(8,128)(2,1)} %get-tuple-element.4), kind=kLoop, calls=%fused_computation | loop fusion | flops 1179648 | bytes 7077888 | tf_op jit(solution)/shard_map/convert_element_type | solution.py:416
